TPU v7x, 32 devices: a whole 2x2x4 slice. The times are simulated.
32 devices in a mesh: gy: 8 (over z, core), gx: 4 (over y, x).
Axes of the slice: x: 2, y: 2, z: 4, core: 2. Of those that a mesh axis runs over, the one named last changes fastest.
Arguments:
- features: bfloat16 [512, 64, 128], P('gy', 'gx'), may hold values from -40 to 40
- attention_gain: float32 [2, 128], replicated, may hold values from 0.25 to 1.75
- triple_weight: bfloat16 [2, 128, 384], replicated, may hold values from -0.5 to 0.5
- output_weight: bfloat16 [2, 128, 128], replicated, may hold values from -0.5 to 0.5
- position_bias: float32 [2, 4, 225], replicated, may hold values from -2 to 262
- hidden_gain: float32 [2, 128], replicated, may hold values from 0.25 to 1.75
- expand_weight: bfloat16 [2, 128, 512], replicated, may hold values from -0.5 to 0.5
- shrink_weight: bfloat16 [2, 512, 128], replicated, may hold values from -0.25 to 0.25
Outputs:
- result: float32 [512, 64, 128], P('gy', 'gx')
All inputs are finite; a program needn't handle non-finite values.
Results may differ from a plain program's by a relative error of at most 0.0033.
Values may be sent and summed in bfloat16 or wider, within the bound.
A program may use at most 64 MiB of HBM per device.

v0:
```python
import functools

import jax
import jax.numpy as jnp
from jax import lax
from jax.experimental import pallas as pl
from jax.experimental.pallas import tpu as pltpu
from jax.sharding import PartitionSpec as P

C = 128
HEADS = 4
WIN = 8
HD = 32
SHIFT = 4
EPSILON = 1e-05
F32 = jnp.float32
BF16 = jnp.bfloat16
GROUP = 2


def layer_norm(values, gain):
    center = values - jnp.mean(values, axis=-1, keepdims=True)
    spread = jnp.mean(center * center, axis=-1, keepdims=True)
    return center * lax.rsqrt(spread + EPSILON) * gain


ERFC = (0.254829592, -0.284496736, 1.421413741, -1.453152027, 1.061405429)
RATE = 0.3275911
POLE = 2**0.5 / RATE
TAIL = [0.5 * c * POLE ** (n + 1) for n, c in enumerate(ERFC)]


def gelu(x):
    a = jnp.abs(x)
    d = a + POLE
    t = pl.reciprocal(d, approx=True)
    t = t * (2.0 - d * t)
    poly = TAIL[4] * t + TAIL[3]
    for coef in TAIL[2::-1]:
        poly = poly * t + coef
    gauss = jnp.exp2((x * x) * (-0.5 * 1.4426950408889634))
    return jnp.maximum(x, 0.0) - (a * t) * (poly * gauss)


def window_pair(triple, bias, second, heads):
    triple = triple.reshape(WIN, 2 * WIN, 3 * C)
    query = triple[:, :, :C].reshape(2 * WIN * WIN, C)
    zero = jnp.zeros_like(query)
    query = jnp.concatenate(
        [jnp.where(second, zero, query), jnp.where(second, query, zero)], axis=1
    ).astype(BF16)
    keys, values = [], []
    for w in range(2):
        part = triple[:, w * WIN : (w + 1) * WIN, C:].reshape(WIN * WIN, 2 * C).astype(BF16)
        keys.append(jnp.concatenate([part[:, :C] * m for m in heads], axis=0))
        values.append(jnp.concatenate([part[:, C:] * m for m in heads], axis=0))
    keys = jnp.concatenate(keys, axis=1)
    values = jnp.concatenate(values, axis=1)
    scores = lax.dot_general(keys, query, (((1,), (1,)), ((), ())), preferred_element_type=F32)
    scores = (scores * HD ** (-0.5) + bias).reshape(HEADS, WIN * WIN, 2 * WIN * WIN)
    powers = jnp.exp(scores - jnp.max(scores, axis=1, keepdims=True))
    probs = powers * (1.0 / jnp.sum(powers, axis=1, keepdims=True))
    probs = probs.reshape(HEADS * WIN * WIN, 2 * WIN * WIN).astype(BF16)
    both = lax.dot_general(probs, values, (((0,), (0,)), ((), ())), preferred_element_type=F32)
    return jnp.where(second, both[:, C:], both[:, :C]).astype(BF16)


def kernel(
    ny, nx, height, breadth,
    feat_in, again_in, tw_in, ow_in, table_in, hgain_in, ew_in, sw_in, out_ref,
    feat, again, tw, ow, table, hgain, ew, sw, out,
    first, ext, back, bias, cs, cr, bcs, bcr, rs, rr, brs, brr, ds, dr, bds, bdr,
    ssem, rsem, isem, osem,
):
    loads = [
        pltpu.make_async_copy(src, dst, isem.at[k])
        for k, (src, dst) in enumerate(
            [
                (table_in, table), (feat_in, feat), (again_in, again), (tw_in, tw),
                (ow_in, ow), (hgain_in, hgain), (ew_in, ew), (sw_in, sw),
            ]
        )
    ]
    for load in loads:
        load.start()
    gy, gx = lax.axis_index("gy"), lax.axis_index("gx")
    up, down = lax.rem(gy + ny - 1, ny), lax.rem(gy + 1, ny)
    left, right = lax.rem(gx + nx - 1, nx), lax.rem(gx + 1, nx)
    barrier = pltpu.get_barrier_semaphore()
    around = [(up, gx), (gy, left), (up, left), (down, gx), (gy, right), (down, right)]
    for who in around:
        pl.semaphore_signal(barrier, inc=1, device_id=who, device_id_type=pl.DeviceIdType.MESH)

    jj = lax.broadcasted_iota(jnp.int32, (WIN, 2 * WIN * WIN), 0)
    lane = lax.broadcasted_iota(jnp.int32, (WIN, 2 * WIN * WIN), 1)
    col_cut = ((jj >= SHIFT) != (lane % WIN >= SHIFT)) & (lane % (2 * WIN) >= WIN) & (gx == nx - 1)
    extent = 2 * WIN - 1
    entry = lax.broadcasted_iota(jnp.int32, (extent * extent, 4 * WIN * WIN), 0)
    place = lax.broadcasted_iota(jnp.int32, (extent * extent, 4 * WIN * WIN), 1)
    pick = jnp.where(
        (entry == place // (2 * WIN) * extent + place % (2 * WIN)) & (place % (2 * WIN) < extent), 1.0, 0.0
    )
    first_half = lax.broadcasted_iota(jnp.int32, (WIN, 4 * WIN * WIN), 1) % (2 * WIN) < WIN
    loads[0].wait()
    spread_rows = [
        jnp.dot(table[b], pick, precision=lax.Precision.HIGHEST, preferred_element_type=F32) for b in range(2)
    ]
    for b in range(2):
        for h in range(HEADS):
            row = jnp.broadcast_to(spread_rows[b][h : h + 1], (WIN, 4 * WIN * WIN))
            rows = jnp.where(
                first_half,
                pltpu.roll(row, 4 * WIN * WIN - WIN + 1, 1, stride=1, stride_axis=0),
                pltpu.roll(row, 1, 1, stride=1, stride_axis=0),
            )
            for y in range(WIN):
                at = (WIN - 1 - y) * 2 * WIN
                piece = rows[:, at : at + 2 * WIN * WIN]
                spot = slice(h * 64 + y * WIN, h * 64 + (y + 1) * WIN)
                if b == 0:
                    bias[0, spot] = piece
                else:
                    row_cut = ((lane >= SHIFT * 2 * WIN) != (y >= SHIFT)) & (gy == ny - 1)
                    bias[1, spot] = piece + jnp.where(col_cut, -100.0, 0.0)
                    bias[2, spot] = piece + jnp.where(col_cut | row_cut, -100.0, 0.0)

    token = lax.broadcasted_iota(jnp.int32, (2 * WIN * WIN, C), 0)
    second = token % (2 * WIN) >= WIN
    channel = lax.broadcasted_iota(jnp.int32, (1, C), 1)
    heads = [jnp.where(channel // HD == h, 1.0, 0.0).astype(BF16) for h in range(HEADS)]
    bands = height // WIN
    band = 2 * WIN * WIN
    group = GROUP
    groups = bands // group
    tall = group * WIN

    def dot(a, b):
        return jnp.dot(a, b, preferred_element_type=F32)

    def spots(i):
        return [i * group + k for k in range(group)]

    def ffn(z, b):
        normed = layer_norm(z, hgain[b : b + 1]).astype(BF16)
        hidden = gelu(dot(normed, ew[b])).astype(BF16)
        return z + dot(hidden, sw[b])

    def block0(i, carry):
        places = spots(i)
        z = jnp.concatenate(
            [feat[pl.ds(r * WIN, WIN), pl.ds(0, 2 * WIN), :].reshape(band, C) for r in places], axis=0
        ).astype(F32)
        triple = dot(layer_norm(z, again[0:1]).astype(BF16), tw[0])
        ctx = [window_pair(triple[k * band : (k + 1) * band], bias[0], second, heads) for k in range(group)]
        branch = dot(jnp.concatenate(ctx, axis=0), ow[0]).astype(BF16).astype(F32)
        z = ffn(z + branch, 0)
        normed = layer_norm(z, again[1:2])
        for k, r in enumerate(places):
            spot = (pl.ds(r * WIN, WIN), pl.ds(0, 2 * WIN), slice(None))
            first[spot] = z[k * band : (k + 1) * band].reshape(WIN, 2 * WIN, C)
            ext[spot] = normed[k * band : (k + 1) * band].reshape(WIN, 2 * WIN, C)
        return carry

    def remote(src, dst, k, who):
        return pltpu.make_async_remote_copy(
            src_ref=src, dst_ref=dst, send_sem=ssem.at[k], recv_sem=rsem.at[k],
            device_id=who, device_id_type=pl.DeviceIdType.MESH,
        )

    def column(g):
        return remote(cs.at[g], cr.at[g], g, (gy, left))

    def column_back(g):
        return remote(bcs.at[g], bcr.at[g], groups + g, (gy, right))

    strips = [
        remote(rs, rr, 2 * groups, (up, gx)), remote(ds, dr, 2 * groups + 1, (up, left)),
        remote(brs, brr, 2 * groups + 2, (down, gx)), remote(bds, bdr, 2 * groups + 3, (down, right)),
    ]
    half = tall // 2

    def pack(ref, r0, c0):
        low = ref[pl.ds(r0, half), c0 : c0 + SHIFT, :]
        high = ref[pl.ds(r0 + half, half), c0 : c0 + SHIFT, :]
        return jnp.concatenate([low, high], axis=1).reshape(half * WIN, C).astype(BF16)

    def unpack(ref, r0, c0, buf):
        both = buf.astype(F32).reshape(half, WIN, C)
        ref[pl.ds(r0, half), c0 : c0 + SHIFT, :] = both[:, :SHIFT]
        ref[pl.ds(r0 + half, half), c0 : c0 + SHIFT, :] = both[:, SHIFT:]

    for load in loads[1:]:
        load.wait()

    def step0(i, carry):
        g = lax.rem(groups - i, groups)
        block0(g, carry)
        cs[g] = pack(ext, g * tall, 0)

        @pl.when(i == 0)
        def _():
            rs[...] = ext[0:SHIFT, 0:breadth, :].reshape(SHIFT * breadth, C).astype(BF16)
            ds[...] = ext[0:SHIFT, 0:WIN, :].reshape(SHIFT * WIN, C).astype(BF16)
            pl.semaphore_wait(barrier, 6)
            strips[0].start()
            strips[1].start()

        column(g).start()
        return carry

    lax.fori_loop(0, groups, step0, 0)

    def block1(i, carry):
        places = spots(i)
        x = jnp.concatenate(
            [
                ext[pl.ds(r * WIN + SHIFT, WIN), pl.ds(SHIFT, 2 * WIN), :].reshape(band, C)
                for r in places
            ],
            axis=0,
        ).astype(BF16)
        triple = dot(x, tw[1])
        ctx = [
            window_pair(
                triple[k * band : (k + 1) * band],
                bias[jnp.where(r == bands - 1, 2, 1)],
                second, heads,
            )
            for k, r in enumerate(places)
        ]
        branch = dot(jnp.concatenate(ctx, axis=0), ow[1])
        for k, r in enumerate(places):
            back[pl.ds(r * WIN + SHIFT, WIN), pl.ds(SHIFT, 2 * WIN), :] = branch[
                k * band : (k + 1) * band
            ].reshape(WIN, 2 * WIN, C)
        return carry

    def step1(i, carry):
        g = groups - 1 - i

        @pl.when(i == 0)
        def _():
            strips[0].wait()
            strips[1].wait()
            ext[height : height + SHIFT, 0:breadth, :] = rr[...].astype(F32).reshape(SHIFT, breadth, C)
            ext[height : height + SHIFT, breadth : breadth + SHIFT, :] = (
                dr[...].astype(F32).reshape(SHIFT, WIN, C)[:, :SHIFT]
            )

        column(g).wait()
        unpack(ext, g * tall, breadth, cr[g])
        block1(g, carry)
        bcs[g] = pack(back, g * tall + SHIFT, breadth)
        column_back(g).start()

        @pl.when(i == 0)
        def _():
            brs[...] = back[height : height + SHIFT, 0:breadth, :].reshape(SHIFT * breadth, C).astype(BF16)
            bds[...] = (
                back[height : height + SHIFT, breadth : breadth + WIN, :].reshape(SHIFT * WIN, C).astype(BF16)
            )
            strips[2].start()
            strips[3].start()

        return carry

    lax.fori_loop(0, groups, step1, 0)

    def arrive(g):
        column_back(g).wait()
        unpack(back, g * tall + SHIFT, 0, bcr[g])

    def tail(i, carry):
        places = spots(i)
        z = jnp.concatenate(
            [
                (
                    first[pl.ds(r * WIN, WIN), pl.ds(0, 2 * WIN), :]
                    + back[pl.ds(r * WIN, WIN), pl.ds(0, 2 * WIN), :].astype(BF16).astype(F32)
                ).reshape(band, C)
                for r in places
            ],
            axis=0,
        )
        z = ffn(z, 1)
        for k, r in enumerate(places):
            out[pl.ds(r * WIN, WIN), pl.ds(0, 2 * WIN), :] = z[k * band : (k + 1) * band].reshape(
                WIN, 2 * WIN, C
            )
        return carry

    def store(g):
        rows = pl.ds(pl.multiple_of(g * tall, tall), tall)
        return pltpu.make_async_copy(out.at[rows], out_ref.at[rows], osem.at[g])

    def step2(i, carry):
        g = groups - 1 - i

        @pl.when(i == 0)
        def _():
            arrive(g)

        @pl.when(g > 0)
        def _():
            arrive(g - 1)

        @pl.when(g == 0)
        def _():
            strips[2].wait()
            strips[3].wait()
            back[0:SHIFT, 0:breadth, :] = brr[...].astype(F32).reshape(SHIFT, breadth, C)
            back[0:SHIFT, 0:SHIFT, :] = bdr[...].astype(F32).reshape(SHIFT, WIN, C)[:, :SHIFT]

        tail(g, carry)
        store(g).start()
        return carry

    lax.fori_loop(0, groups, step2, 0)
    for g in range(groups):
        store(g).wait()


def on_device(ny, nx, *operands):
    height, breadth, _ = operands[0].shape
    groups = height // (GROUP * WIN)
    col, row, corner = (groups, GROUP * WIN * SHIFT, C), (SHIFT * breadth, C), (SHIFT * WIN, C)
    hbm = pl.BlockSpec(memory_space=pl.ANY)
    return pl.pallas_call(
        functools.partial(kernel, ny, nx, height, breadth),
        out_shape=jax.ShapeDtypeStruct((height, breadth, C), F32),
        in_specs=[hbm] * len(operands),
        out_specs=hbm,
        scratch_shapes=[pltpu.VMEM(x.shape, x.dtype) for x in operands]
        + [
            pltpu.VMEM((height, breadth, C), F32),
            pltpu.VMEM((height, breadth, C), F32),
            pltpu.VMEM((height + SHIFT, breadth + WIN, C), F32),
            pltpu.VMEM((height + SHIFT, breadth + WIN, C), F32),
            pltpu.VMEM((3, HEADS * WIN * WIN, 2 * WIN * WIN), F32),
        ]
        + [pltpu.VMEM(shape, BF16) for shape in [col] * 4 + [row] * 4 + [corner] * 4]
        + [
            pltpu.SemaphoreType.DMA((2 * groups + 4,)),
            pltpu.SemaphoreType.DMA((2 * groups + 4,)),
            pltpu.SemaphoreType.DMA((len(operands),)),
            pltpu.SemaphoreType.DMA((groups,)),
        ],
        compiler_params=pltpu.CompilerParams(
            collective_id=0, has_side_effects=True, vmem_limit_bytes=48 * 1024 * 1024
        ),
        cost_estimate=pl.CostEstimate(flops=10**9, bytes_accessed=2 * 10**6, transcendentals=10**6),
    )(*operands)


def solution(mesh):
    return jax.shard_map(
        functools.partial(on_device, mesh.shape["gy"], mesh.shape["gx"]),
        mesh=mesh,
        in_specs=(P("gy", "gx", None), P(), P(), P(), P(), P(), P(), P()),
        out_specs=P("gy", "gx", None),
        check_vma=False,
    )
```

profile of v0, /device:TPU:0, one launch (start us, length us, event | category | flops | bytes accessed | tf_op | source)
XLA Modules:
  0.0 31.4 jit_solution(5456078316171334976)
XLA Ops:
  0.0 0.0 copy-start
  0.0 0.9 %copy-done = bf16[64,16,128]{2,1,0:T(8,128)(2,1)S(1)} copy-done((bf16[64,16,128]{2,1,0:T(8,128)(2,1)S(1)}, bf16[64,16,128]{2,1,0:T(8,128)(2,1)}, u32[]{:S(2)}) %copy-start) | copy-done | bytes 262168
  1.0 0.0 copy-start.1
  1.0 0.9 %copy-done.1 = bf16[2,128,512]{2,1,0:T(8,128)(2,1)S(1)} copy-done((bf16[2,128,512]{2,1,0:T(8,128)(2,1)S(1)}, bf16[2,128,512]{2,1,0:T(8,128)(2,1)}, u32[]{:S(2)}) %copy-start.1) | copy-done | bytes 262168
  1.9 0.0 copy-start.2
  1.9 0.9 %copy-done.2 = bf16[2,512,128]{2,1,0:T(8,128)(2,1)S(1)} copy-done((bf16[2,512,128]{2,1,0:T(8,128)(2,1)S(1)}, bf16[2,512,128]{2,1,0:T(8,128)(2,1)}, u32[]{:S(2)}) %copy-start.2) | copy-done | bytes 262168
  2.9 0.0 copy-start.3
  2.9 0.9 %copy-done.3 = bf16[2,128,384]{2,1,0:T(8,128)(2,1)S(1)} copy-done((bf16[2,128,384]{2,1,0:T(8,128)(2,1)S(1)}, bf16[2,128,384]{2,1,0:T(8,128)(2,1)}, u32[]{:S(2)}) %copy-start.3) | copy-done | bytes 196632
  3.8 0.0 copy-start.4
  3.8 0.8 %copy-done.4 = bf16[2,128,128]{2,1,0:T(8,128)(2,1)S(1)} copy-done((bf16[2,128,128]{2,1,0:T(8,128)(2,1)S(1)}, bf16[2,128,128]{2,1,0:T(8,128)(2,1)}, u32[]{:S(2)}) %copy-start.4) | copy-done | bytes 65560
  4.6 0.0 copy-start.5
  4.6 0.7 %copy-done.5 = f32[2,4,225]{2,1,0:T(4,128)S(1)} copy-done((f32[2,4,225]{2,1,0:T(4,128)S(1)}, f32[2,4,225]{2,1,0:T(4,128)}, u32[]{:S(2)}) %copy-start.5) | copy-done | bytes 7224
  5.3 0.0 copy-start.6
  5.3 0.7 %copy-done.6 = f32[2,128]{1,0:T(2,128)S(1)} copy-done((f32[2,128]{1,0:T(2,128)S(1)}, f32[2,128]{1,0:T(2,128)}, u32[]{:S(2)}) %copy-start.6) | copy-done | bytes 1048
  6.0 0.0 copy-start.7
  6.0 0.7 %copy-done.7 = f32[2,128]{1,0:T(2,128)S(1)} copy-done((f32[2,128]{1,0:T(2,128)S(1)}, f32[2,128]{1,0:T(2,128)}, u32[]{:S(2)}) %copy-start.7) | copy-done | bytes 1048
  6.7 24.0 %shard_map.82 = f32[64,16,128]{2,1,0:T(8,128)S(1)} custom-call(bf16[64,16,128]{2,1,0:T(8,128)(2,1)S(1)} %copy-done, f32[2,128]{1,0:T(2,128)S(1)} %copy-done.6, bf16[2,128,384]{2,1,0:T(8,128)(2,1)S(1)} %copy-done.3, bf16[2,128,128]{2,1,0:T(8,128)(2,1)S(1)} %copy-done.4, f32[2,4,225]{2,1,0:T(4,128)S(1)} %copy-done.5, f32[2,128]{1,0:T(2,128)S(1)} %copy-done.7, ...), custom_call_target="tpu_custom_call" | custom-call | flops 1000000000 | bytes 2000000 | tf_op jit(solution)/shard_map/pallas_call | solution.py:328
  30.6 0.8 %copy.10 = f32[64,16,128]{2,1,0:T(8,128)} copy(f32[64,16,128]{2,1,0:T(8,128)S(1)} %shard_map.82) | data formatting | bytes 1048576
Async XLA Ops:
  0.0 0.9 %copy-start = (bf16[64,16,128]{2,1,0:T(8,128)(2,1)S(1)}, bf16[64,16,128]{2,1,0:T(8,128)(2,1)}, u32[]{:S(2)}) copy-start(bf16[64,16,128]{2,1,0:T(8,128)(2,1)} %feat_in.1) | copy-start | bytes 786436
  1.0 0.9 %copy-start.1 = (bf16[2,128,512]{2,1,0:T(8,128)(2,1)S(1)}, bf16[2,128,512]{2,1,0:T(8,128)(2,1)}, u32[]{:S(2)}) copy-start(bf16[2,128,512]{2,1,0:T(8,128)(2,1)} %ew_in.1) | copy-start | bytes 786436
  1.9 0.9 %copy-start.2 = (bf16[2,512,128]{2,1,0:T(8,128)(2,1)S(1)}, bf16[2,512,128]{2,1,0:T(8,128)(2,1)}, u32[]{:S(2)}) copy-start(bf16[2,512,128]{2,1,0:T(8,128)(2,1)} %sw_in.1) | copy-start | bytes 786436
  2.9 0.9 %copy-start.3 = (bf16[2,128,384]{2,1,0:T(8,128)(2,1)S(1)}, bf16[2,128,384]{2,1,0:T(8,128)(2,1)}, u32[]{:S(2)}) copy-start(bf16[2,128,384]{2,1,0:T(8,128)(2,1)} %tw_in.1) | copy-start | bytes 589828
  3.8 0.8 %copy-start.4 = (bf16[2,128,128]{2,1,0:T(8,128)(2,1)S(1)}, bf16[2,128,128]{2,1,0:T(8,128)(2,1)}, u32[]{:S(2)}) copy-start(bf16[2,128,128]{2,1,0:T(8,128)(2,1)} %ow_in.1) | copy-start | bytes 196612
  4.6 0.7 %copy-start.5 = (f32[2,4,225]{2,1,0:T(4,128)S(1)}, f32[2,4,225]{2,1,0:T(4,128)}, u32[]{:S(2)}) copy-start(f32[2,4,225]{2,1,0:T(4,128)} %table_in.1) | copy-start | bytes 21604
  5.3 0.7 %copy-start.6 = (f32[2,128]{1,0:T(2,128)S(1)}, f32[2,128]{1,0:T(2,128)}, u32[]{:S(2)}) copy-start(f32[2,128]{1,0:T(2,128)} %again_in.1) | copy-start | bytes 3076
  6.0 0.7 %copy-start.7 = (f32[2,128]{1,0:T(2,128)S(1)}, f32[2,128]{1,0:T(2,128)}, u32[]{:S(2)}) copy-start(f32[2,128]{1,0:T(2,128)} %hgain_in.1) | copy-start | bytes 3076
where the time goes:
time: 31.8 us; the launch traced here: 31.4 us
  Pallas kernels  24 us (75%)
  local copies, waits for them, and re-layouts  7.46 us (23%)
    pallas_call x1, Pallas kernels, on_device(): pl.pallas_call(functools.partial(kernel, ny, nx, height, breadth), out_sh...  24 us
    unnamed x17, local copies, waits for them, and re-layouts  7.46 us

commit v1 on v0

--- a/solution.py
+++ b/solution.py
@@ -93,14 +93,14 @@
 
     jj = lax.broadcasted_iota(jnp.int32, (WIN, 2 * WIN * WIN), 0)
     lane = lax.broadcasted_iota(jnp.int32, (WIN, 2 * WIN * WIN), 1)
-    col_cut = ((jj >= SHIFT) != (lane % WIN >= SHIFT)) & (lane % (2 * WIN) >= WIN) & (gx == nx - 1)
+    col_cut = ((jj >= SHIFT) != (lane & 7 >= SHIFT)) & (lane & 15 >= WIN) & (gx == nx - 1)
     extent = 2 * WIN - 1
     entry = lax.broadcasted_iota(jnp.int32, (extent * extent, 4 * WIN * WIN), 0)
     place = lax.broadcasted_iota(jnp.int32, (extent * extent, 4 * WIN * WIN), 1)
     pick = jnp.where(
-        (entry == place // (2 * WIN) * extent + place % (2 * WIN)) & (place % (2 * WIN) < extent), 1.0, 0.0
+        (entry == (place >> 4) * extent + (place & 15)) & ((place & 15) < extent), 1.0, 0.0
     )
-    first_half = lax.broadcasted_iota(jnp.int32, (WIN, 4 * WIN * WIN), 1) % (2 * WIN) < WIN
+    first_half = lax.broadcasted_iota(jnp.int32, (WIN, 4 * WIN * WIN), 1) & 15 < WIN
     loads[0].wait()
     spread_rows = [
         jnp.dot(table[b], pick, precision=lax.Precision.HIGHEST, preferred_element_type=F32) for b in range(2)
@@ -125,9 +125,9 @@
                     bias[2, spot] = piece + jnp.where(col_cut | row_cut, -100.0, 0.0)
 
     token = lax.broadcasted_iota(jnp.int32, (2 * WIN * WIN, C), 0)
-    second = token % (2 * WIN) >= WIN
+    second = token & 15 >= WIN
     channel = lax.broadcasted_iota(jnp.int32, (1, C), 1)
-    heads = [jnp.where(channel // HD == h, 1.0, 0.0).astype(BF16) for h in range(HEADS)]
+    heads = [jnp.where(channel >> 5 == h, 1.0, 0.0).astype(BF16) for h in range(HEADS)]
     bands = height // WIN
     band = 2 * WIN * WIN
     group = GROUP
@@ -137,8 +137,10 @@
     def dot(a, b):
         return jnp.dot(a, b, preferred_element_type=F32)
 
-    def spots(i):
-        return [i * group + k for k in range(group)]
+    wide = 2 * group
+
+    def spots(first_band, count):
+        return [lax.rem(first_band + k, bands) for k in range(count)]
 
     def ffn(z, b):
         normed = layer_norm(z, hgain[b : b + 1]).astype(BF16)
@@ -146,12 +148,12 @@
         return z + dot(hidden, sw[b])
 
     def block0(i, carry):
-        places = spots(i)
+        places = spots(i * wide, wide)
         z = jnp.concatenate(
             [feat[pl.ds(r * WIN, WIN), pl.ds(0, 2 * WIN), :].reshape(band, C) for r in places], axis=0
         ).astype(F32)
         triple = dot(layer_norm(z, again[0:1]).astype(BF16), tw[0])
-        ctx = [window_pair(triple[k * band : (k + 1) * band], bias[0], second, heads) for k in range(group)]
+        ctx = [window_pair(triple[k * band : (k + 1) * band], bias[0], second, heads) for k in range(wide)]
         branch = dot(jnp.concatenate(ctx, axis=0), ow[0]).astype(BF16).astype(F32)
         z = ffn(z + branch, 0)
         normed = layer_norm(z, again[1:2])
@@ -193,9 +195,9 @@
         load.wait()
 
     def step0(i, carry):
-        g = lax.rem(groups - i, groups)
-        block0(g, carry)
-        cs[g] = pack(ext, g * tall, 0)
+        block0(i, carry)
+        for k in range(2):
+            cs[2 * i + k] = pack(ext, (2 * i + k) * tall, 0)
 
         @pl.when(i == 0)
         def _():
@@ -205,13 +207,14 @@
             strips[0].start()
             strips[1].start()
 
-        column(g).start()
-        return carry
-
-    lax.fori_loop(0, groups, step0, 0)
+        for k in range(2):
+            column(2 * i + k).start()
+        return carry
+
+    lax.fori_loop(0, groups // 2, step0, 0)
 
     def block1(i, carry):
-        places = spots(i)
+        places = spots(i * group, group)
         x = jnp.concatenate(
             [
                 ext[pl.ds(r * WIN + SHIFT, WIN), pl.ds(SHIFT, 2 * WIN), :].reshape(band, C)
@@ -235,10 +238,20 @@
             ].reshape(WIN, 2 * WIN, C)
         return carry
 
-    def step1(i, carry):
-        g = groups - 1 - i
-
-        @pl.when(i == 0)
+    def enter(g):
+        column(g).wait()
+        unpack(ext, g * tall, breadth, cr[g])
+
+    def step1(g, carry):
+        @pl.when(g == 0)
+        def _():
+            enter(g)
+
+        @pl.when(g < groups - 1)
+        def _():
+            enter(g + 1)
+
+        @pl.when(g == groups - 1)
         def _():
             strips[0].wait()
             strips[1].wait()
@@ -247,13 +260,11 @@
                 dr[...].astype(F32).reshape(SHIFT, WIN, C)[:, :SHIFT]
             )
 
-        column(g).wait()
-        unpack(ext, g * tall, breadth, cr[g])
         block1(g, carry)
         bcs[g] = pack(back, g * tall + SHIFT, breadth)
         column_back(g).start()
 
-        @pl.when(i == 0)
+        @pl.when(g == groups - 1)
         def _():
             brs[...] = back[height : height + SHIFT, 0:breadth, :].reshape(SHIFT * breadth, C).astype(BF16)
             bds[...] = (
@@ -271,7 +282,7 @@
         unpack(back, g * tall + SHIFT, 0, bcr[g])
 
     def tail(i, carry):
-        places = spots(i)
+        places = spots(i * wide + group, wide)
         z = jnp.concatenate(
             [
                 (
@@ -294,28 +305,29 @@
         return pltpu.make_async_copy(out.at[rows], out_ref.at[rows], osem.at[g])
 
     def step2(i, carry):
-        g = groups - 1 - i
-
         @pl.when(i == 0)
         def _():
-            arrive(g)
-
-        @pl.when(g > 0)
-        def _():
-            arrive(g - 1)
-
-        @pl.when(g == 0)
+            arrive(0)
+
+        arrive(2 * i + 1)
+
+        @pl.when(i < groups // 2 - 1)
+        def _():
+            arrive(2 * i + 2)
+
+        @pl.when(i == groups // 2 - 1)
         def _():
             strips[2].wait()
             strips[3].wait()
             back[0:SHIFT, 0:breadth, :] = brr[...].astype(F32).reshape(SHIFT, breadth, C)
             back[0:SHIFT, 0:SHIFT, :] = bdr[...].astype(F32).reshape(SHIFT, WIN, C)[:, :SHIFT]
 
-        tail(g, carry)
-        store(g).start()
-        return carry
-
-    lax.fori_loop(0, groups, step2, 0)
+        tail(i, carry)
+        store(2 * i + 1).start()
+        store(lax.rem(2 * i + 2, groups)).start()
+        return carry
+
+    lax.fori_loop(0, groups // 2, step2, 0)
     for g in range(groups):
         store(g).wait()
 
@@ -346,7 +358,7 @@
             pltpu.SemaphoreType.DMA((groups,)),
         ],
         compiler_params=pltpu.CompilerParams(
-            collective_id=0, has_side_effects=True, vmem_limit_bytes=48 * 1024 * 1024
+            collective_id=0, has_side_effects=True, vmem_limit_bytes=64 * 1024 * 1024
         ),
         cost_estimate=pl.CostEstimate(flops=10**9, bytes_accessed=2 * 10**6, transcendentals=10**6),
     )(*operands)

time: 31.8 us -> 24.1 us (0.76)
  local copies, waits for them, and re-layouts: 7.46 us -> 1.87 us
  Pallas kernels: 24 us -> 22 us
    unnamed x17 -> x1, local copies, waits for them, and re-layouts: 7.46 us -> 1.87 us
    pallas_call x1, Pallas kernels: 24 us -> 22 us  [on_device(): pl.pallas_call(functools.partial(kernel, ny, nx, height, breadth), out_sh...]
where the time goes in v1:
time: 24.1 us; the launch traced here: 23.9 us
  Pallas kernels  22 us (91%)
  local copies, waits for them, and re-layouts  1.87 us (8%)
    pallas_call x1, Pallas kernels, on_device(): pl.pallas_call(functools.partial(kernel, ny, nx, height, breadth), out_sh...  22 us
    unnamed x1, local copies, waits for them, and re-layouts  1.87 us

profile of v1, /device:TPU:0, one launch (start us, length us, event | category | flops | bytes accessed | tf_op | source)
XLA Modules:
  0.0 23.9 jit_solution(11938870949421189299)
XLA Ops:
  0.0 22.0 %shard_map.82 = f32[64,16,128]{2,1,0:T(8,128)} custom-call(bf16[64,16,128]{2,1,0:T(8,128)(2,1)} %feat_in.1, f32[2,128]{1,0:T(2,128)} %again_in.1, bf16[2,128,384]{2,1,0:T(8,128)(2,1)} %tw_in.1, bf16[2,128,128]{2,1,0:T(8,128)(2,1)} %ow_in.1, f32[2,4,225]{2,1,0:T(4,128)} %table_in.1, f32[2,128]{1,0:T(2,128)} %hgain_in.1, bf16[2,128,512]{2,1,0:T(8,128)(2,1)} %ew_in.1, ...), custom_call_target="tpu_custom_call" | custom-call | flops 1000000000 | bytes 2000000 | tf_op jit(solution)/shard_map/pallas_call | solution.py:340
  22.0 1.9 %copy.10 = f32[64,16,128]{2,1,0:T(8,128)} copy(f32[64,16,128]{2,1,0:T(8,128)} %shard_map.82) | data formatting | bytes 1048576

commit v2 on v1

--- a/solution.py
+++ b/solution.py
@@ -293,7 +293,6 @@
             ],
             axis=0,
         )
-        z = ffn(z, 1)
         for k, r in enumerate(places):
             out[pl.ds(r * WIN, WIN), pl.ds(0, 2 * WIN), :] = z[k * band : (k + 1) * band].reshape(
                 WIN, 2 * WIN, C
@@ -330,6 +329,14 @@
     lax.fori_loop(0, groups // 2, step2, 0)
     for g in range(groups):
         store(g).wait()
+
+
+def finish(z_ref, gain, ew, sw, out):
+    shape = z_ref.shape
+    z = z_ref[...].reshape(-1, C)
+    normed = layer_norm(z, gain[1:2]).astype(BF16)
+    hidden = gelu(jnp.dot(normed, ew[0], preferred_element_type=F32)).astype(BF16)
+    out[...] = (z + jnp.dot(hidden, sw[0], preferred_element_type=F32)).reshape(shape)
 
 
 def on_device(ny, nx, *operands):
@@ -337,7 +344,7 @@
     groups = height // (GROUP * WIN)
     col, row, corner = (groups, GROUP * WIN * SHIFT, C), (SHIFT * breadth, C), (SHIFT * WIN, C)
     hbm = pl.BlockSpec(memory_space=pl.ANY)
-    return pl.pallas_call(
+    middle = pl.pallas_call(
         functools.partial(kernel, ny, nx, height, breadth),
         out_shape=jax.ShapeDtypeStruct((height, breadth, C), F32),
         in_specs=[hbm] * len(operands),
@@ -362,6 +369,21 @@
         ),
         cost_estimate=pl.CostEstimate(flops=10**9, bytes_accessed=2 * 10**6, transcendentals=10**6),
     )(*operands)
+    hidden_gain, expand_weight, shrink_weight = operands[5:]
+    tile = pl.BlockSpec((2 * GROUP * WIN, breadth, C), lambda i: (i, 0, 0))
+    return pl.pallas_call(
+        finish,
+        grid=(height // (2 * GROUP * WIN),),
+        out_shape=jax.ShapeDtypeStruct((height, breadth, C), F32),
+        in_specs=[
+            tile,
+            pl.BlockSpec(hidden_gain.shape, lambda i: (0, 0)),
+            pl.BlockSpec((1, *expand_weight.shape[1:]), lambda i: (1, 0, 0)),
+            pl.BlockSpec((1, *shrink_weight.shape[1:]), lambda i: (1, 0, 0)),
+        ],
+        out_specs=tile,
+        compiler_params=pltpu.CompilerParams(vmem_limit_bytes=64 * 1024 * 1024),
+    )(middle, hidden_gain, expand_weight, shrink_weight)
 
 
 def solution(mesh):

time: 24.1 us -> 25.4 us (1.054)
  Pallas kernels: 22 us -> 25.2 us
  local copies, waits for them, and re-layouts: 1.87 us -> 0 us
    pallas_call x0 -> x1, Pallas kernels: none -> 4.42 us  [on_device(): pl.pallas_call(finish, grid=(height // (2 * GROUP * WIN),), out_shape=jax...]
    unnamed x1 -> x0, local copies, waits for them, and re-layouts: 1.87 us -> none
    pallas_call x1, Pallas kernels: 22 us -> 20.7 us  [on_device(): pl.pallas_call(functools.partial(kernel, ny, nx, height, breadth), out_sh...]
where the time goes in v2:
time: 25.4 us; the launch traced here: 25.2 us
  Pallas kernels  25.2 us (99%)
    pallas_call x1, Pallas kernels, on_device(): pl.pallas_call(functools.partial(kernel, ny, nx, height, breadth), out_sh...  20.7 us
    pallas_call x1, Pallas kernels, on_device(): pl.pallas_call(finish, grid=(height // (2 * GROUP * WIN),), out_shape=jax...  4.42 us

profile of v2, /device:TPU:0, one launch (start us, length us, event | category | flops | bytes accessed | tf_op | source)
XLA Modules:
  0.0 25.2 jit_solution(6134858570755139067)
XLA Ops:
  0.0 20.7 %shard_map.82.z_ref = f32[64,16,128]{2,1,0:T(8,128)} custom-call(bf16[64,16,128]{2,1,0:T(8,128)(2,1)} %feat_in.1, f32[2,128]{1,0:T(2,128)} %again_in.1, bf16[2,128,384]{2,1,0:T(8,128)(2,1)} %tw_in.1, bf16[2,128,128]{2,1,0:T(8,128)(2,1)} %ow_in.1, f32[2,4,225]{2,1,0:T(4,128)} %table_in.1, f32[2,128]{1,0:T(2,128)} %gain.1, bf16[2,128,512]{2,1,0:T(8,128)(2,1)} %ew.1, ...), custom_call_target="tpu_custom_call" | custom-call | flops 1000000000 | bytes 2000000 | tf_op jit(solution)/shard_map/pallas_call | solution.py:347
  20.7 4.4 %shard_map.83 = f32[64,16,128]{2,1,0:T(8,128)} custom-call(f32[64,16,128]{2,1,0:T(8,128)} %shard_map.82.z_ref, f32[2,128]{1,0:T(2,128)} %gain.1, bf16[2,128,512]{2,1,0:T(8,128)(2,1)} %ew.1, bf16[2,512,128]{2,1,0:T(8,128)(2,1)} %sw.1), custom_call_target="tpu_custom_call" | custom-call | tf_op jit(solution)/shard_map/pallas_call | solution.py:374

commit v3 on v1

--- a/solution.py
+++ b/solution.py
@@ -143,9 +143,13 @@
         return [lax.rem(first_band + k, bands) for k in range(count)]
 
     def ffn(z, b):
-        normed = layer_norm(z, hgain[b : b + 1]).astype(BF16)
-        hidden = gelu(dot(normed, ew[b])).astype(BF16)
-        return z + dot(hidden, sw[b])
+        parts = []
+        for k in range(z.shape[0] // band):
+            part = z[k * band : (k + 1) * band]
+            normed = layer_norm(part, hgain[b : b + 1]).astype(BF16)
+            hidden = gelu(dot(normed, ew[b])).astype(BF16)
+            parts.append(part + dot(hidden, sw[b]))
+        return jnp.concatenate(parts, axis=0)
 
     def block0(i, carry):
         places = spots(i * wide, wide)

time: 24.1 us -> 24.9 us (1.033)
  Pallas kernels: 22 us -> 22.9 us
    pallas_call x1, Pallas kernels: 22 us -> 22.9 us  [on_device(): pl.pallas_call(functools.partial(kernel, ny, nx, height, breadth), out_sh...]
where the time goes in v3:
time: 24.9 us; the launch traced here: 24.7 us
  Pallas kernels  22.9 us (92%)
  local copies, waits for them, and re-layouts  1.87 us (8%)
    pallas_call x1, Pallas kernels, on_device(): pl.pallas_call(functools.partial(kernel, ny, nx, height, breadth), out_sh...  22.9 us
    unnamed x1, local copies, waits for them, and re-layouts  1.87 us

profile of v3, /device:TPU:0, one launch (start us, length us, event | category | flops | bytes accessed | tf_op | source)
XLA Modules:
  0.0 24.7 jit_solution(12874980897956296931)
XLA Ops:
  0.0 22.9 %shard_map.82 = f32[64,16,128]{2,1,0:T(8,128)} custom-call(bf16[64,16,128]{2,1,0:T(8,128)(2,1)} %feat_in.1, f32[2,128]{1,0:T(2,128)} %again_in.1, bf16[2,128,384]{2,1,0:T(8,128)(2,1)} %tw_in.1, bf16[2,128,128]{2,1,0:T(8,128)(2,1)} %ow_in.1, f32[2,4,225]{2,1,0:T(4,128)} %table_in.1, f32[2,128]{1,0:T(2,128)} %hgain_in.1, bf16[2,128,512]{2,1,0:T(8,128)(2,1)} %ew_in.1, ...), custom_call_target="tpu_custom_call" | custom-call | flops 1000000000 | bytes 2000000 | tf_op jit(solution)/shard_map/pallas_call | solution.py:344
  22.9 1.9 %copy.10 = f32[64,16,128]{2,1,0:T(8,128)} copy(f32[64,16,128]{2,1,0:T(8,128)} %shard_map.82) | data formatting | bytes 1048576

commit v4 on v1

--- a/solution.py
+++ b/solution.py
@@ -67,10 +67,10 @@
 
 def kernel(
     ny, nx, height, breadth,
-    feat_in, again_in, tw_in, ow_in, table_in, hgain_in, ew_in, sw_in, out_ref,
-    feat, again, tw, ow, table, hgain, ew, sw, out,
+    feat_in, again_in, tw_in, ow_in, table_in, hgain_in, ew_in, sw_in, out,
+    feat, again, tw, ow, table, hgain, ew, sw,
     first, ext, back, bias, cs, cr, bcs, bcr, rs, rr, brs, brr, ds, dr, bds, bdr,
-    ssem, rsem, isem, osem,
+    ssem, rsem, isem,
 ):
     loads = [
         pltpu.make_async_copy(src, dst, isem.at[k])
@@ -300,10 +300,6 @@
             )
         return carry
 
-    def store(g):
-        rows = pl.ds(pl.multiple_of(g * tall, tall), tall)
-        return pltpu.make_async_copy(out.at[rows], out_ref.at[rows], osem.at[g])
-
     def step2(i, carry):
         @pl.when(i == 0)
         def _():
@@ -323,13 +319,9 @@
             back[0:SHIFT, 0:SHIFT, :] = bdr[...].astype(F32).reshape(SHIFT, WIN, C)[:, :SHIFT]
 
         tail(i, carry)
-        store(2 * i + 1).start()
-        store(lax.rem(2 * i + 2, groups)).start()
         return carry
 
     lax.fori_loop(0, groups // 2, step2, 0)
-    for g in range(groups):
-        store(g).wait()
 
 
 def on_device(ny, nx, *operands):
@@ -339,12 +331,11 @@
     hbm = pl.BlockSpec(memory_space=pl.ANY)
     return pl.pallas_call(
         functools.partial(kernel, ny, nx, height, breadth),
-        out_shape=jax.ShapeDtypeStruct((height, breadth, C), F32),
+        out_shape=pltpu.VMEM((height, breadth, C), F32),
         in_specs=[hbm] * len(operands),
-        out_specs=hbm,
+        out_specs=pl.BlockSpec(memory_space=pltpu.VMEM),
         scratch_shapes=[pltpu.VMEM(x.shape, x.dtype) for x in operands]
         + [
-            pltpu.VMEM((height, breadth, C), F32),
             pltpu.VMEM((height, breadth, C), F32),
             pltpu.VMEM((height + SHIFT, breadth + WIN, C), F32),
             pltpu.VMEM((height + SHIFT, breadth + WIN, C), F32),
@@ -355,10 +346,9 @@
             pltpu.SemaphoreType.DMA((2 * groups + 4,)),
             pltpu.SemaphoreType.DMA((2 * groups + 4,)),
             pltpu.SemaphoreType.DMA((len(operands),)),
-            pltpu.SemaphoreType.DMA((groups,)),
         ],
         compiler_params=pltpu.CompilerParams(
-            collective_id=0, has_side_effects=True, vmem_limit_bytes=64 * 1024 * 1024
+            collective_id=0, has_side_effects=True, vmem_limit_bytes=(64 * 1024 - 600) * 1024
         ),
         cost_estimate=pl.CostEstimate(flops=10**9, bytes_accessed=2 * 10**6, transcendentals=10**6),
     )(*operands)

time: 24.1 us -> 22.3 us (0.925)
  local copies, waits for them, and re-layouts: 1.87 us -> 0.8 us
  Pallas kernels: 22 us -> 21.3 us
    unnamed x1, local copies, waits for them, and re-layouts: 1.87 us -> 0.8 us
    pallas_call x1, Pallas kernels: 22 us -> 21.3 us  [on_device(): pl.pallas_call(functools.partial(kernel, ny, nx, height, breadth), out_sh...]
where the time goes in v4:
time: 22.3 us; the launch traced here: 22.1 us
  Pallas kernels  21.3 us (96%)
  local copies, waits for them, and re-layouts  0.8 us (4%)
    pallas_call x1, Pallas kernels, on_device(): pl.pallas_call(functools.partial(kernel, ny, nx, height, breadth), out_sh...  21.3 us
    unnamed x1, local copies, waits for them, and re-layouts  0.8 us

profile of v4, /device:TPU:0, one launch (start us, length us, event | category | flops | bytes accessed | tf_op | source)
XLA Modules:
  0.0 22.1 jit_solution(8749892397144359896)
XLA Ops:
  0.0 21.3 %shard_map.82 = f32[64,16,128]{2,1,0:T(8,128)S(1)} custom-call(bf16[64,16,128]{2,1,0:T(8,128)(2,1)} %feat_in.1, f32[2,128]{1,0:T(2,128)} %again_in.1, bf16[2,128,384]{2,1,0:T(8,128)(2,1)} %tw_in.1, bf16[2,128,128]{2,1,0:T(8,128)(2,1)} %ow_in.1, f32[2,4,225]{2,1,0:T(4,128)} %table_in.1, f32[2,128]{1,0:T(2,128)} %hgain_in.1, bf16[2,128,512]{2,1,0:T(8,128)(2,1)} %ew_in.1, ...), custom_call_target="tpu_custom_call" | custom-call | flops 1000000000 | bytes 2000000 | tf_op jit(solution)/shard_map/pallas_call | solution.py:332
  21.3 0.8 %copy.10 = f32[64,16,128]{2,1,0:T(8,128)} copy(f32[64,16,128]{2,1,0:T(8,128)S(1)} %shard_map.82) | data formatting | bytes 1048576

commit v5 on v4

--- a/solution.py
+++ b/solution.py
@@ -42,12 +42,11 @@
     return jnp.maximum(x, 0.0) - (a * t) * (poly * gauss)
 
 
-def window_pair(triple, bias, second, heads):
+def window_pair(triple, turned, bias, second, rows_second, heads):
     triple = triple.reshape(WIN, 2 * WIN, 3 * C)
-    query = triple[:, :, :C].reshape(2 * WIN * WIN, C)
-    zero = jnp.zeros_like(query)
+    zero = jnp.zeros_like(turned)
     query = jnp.concatenate(
-        [jnp.where(second, zero, query), jnp.where(second, query, zero)], axis=1
+        [jnp.where(second, zero, turned), jnp.where(second, turned, zero)], axis=0
     ).astype(BF16)
     keys, values = [], []
     for w in range(2):
@@ -56,13 +55,13 @@
         values.append(jnp.concatenate([part[:, C:] * m for m in heads], axis=0))
     keys = jnp.concatenate(keys, axis=1)
     values = jnp.concatenate(values, axis=1)
-    scores = lax.dot_general(keys, query, (((1,), (1,)), ((), ())), preferred_element_type=F32)
+    scores = jnp.dot(keys, query, preferred_element_type=F32)
     scores = (scores * HD ** (-0.5) + bias).reshape(HEADS, WIN * WIN, 2 * WIN * WIN)
     powers = jnp.exp(scores - jnp.max(scores, axis=1, keepdims=True))
     probs = powers * (1.0 / jnp.sum(powers, axis=1, keepdims=True))
     probs = probs.reshape(HEADS * WIN * WIN, 2 * WIN * WIN).astype(BF16)
     both = lax.dot_general(probs, values, (((0,), (0,)), ((), ())), preferred_element_type=F32)
-    return jnp.where(second, both[:, C:], both[:, :C]).astype(BF16)
+    return jnp.where(rows_second, both[:, C:], both[:, :C]).astype(BF16)
 
 
 def kernel(
@@ -125,7 +124,8 @@
                     bias[2, spot] = piece + jnp.where(col_cut | row_cut, -100.0, 0.0)
 
     token = lax.broadcasted_iota(jnp.int32, (2 * WIN * WIN, C), 0)
-    second = token & 15 >= WIN
+    rows_second = token & 15 >= WIN
+    second = lax.broadcasted_iota(jnp.int32, (C, 2 * WIN * WIN), 1) & 15 >= WIN
     channel = lax.broadcasted_iota(jnp.int32, (1, C), 1)
     heads = [jnp.where(channel >> 5 == h, 1.0, 0.0).astype(BF16) for h in range(HEADS)]
     bands = height // WIN
@@ -153,7 +153,14 @@
             [feat[pl.ds(r * WIN, WIN), pl.ds(0, 2 * WIN), :].reshape(band, C) for r in places], axis=0
         ).astype(F32)
         triple = dot(layer_norm(z, again[0:1]).astype(BF16), tw[0])
-        ctx = [window_pair(triple[k * band : (k + 1) * band], bias[0], second, heads) for k in range(wide)]
+        turned = triple[:, :C].T
+        ctx = [
+            window_pair(
+                triple[k * band : (k + 1) * band], turned[:, k * band : (k + 1) * band], bias[0],
+                second, rows_second, heads,
+            )
+            for k in range(wide)
+        ]
         branch = dot(jnp.concatenate(ctx, axis=0), ow[0]).astype(BF16).astype(F32)
         z = ffn(z + branch, 0)
         normed = layer_norm(z, again[1:2])
@@ -223,11 +230,11 @@
             axis=0,
         ).astype(BF16)
         triple = dot(x, tw[1])
+        turned = triple[:, :C].T
         ctx = [
             window_pair(
-                triple[k * band : (k + 1) * band],
-                bias[jnp.where(r == bands - 1, 2, 1)],
-                second, heads,
+                triple[k * band : (k + 1) * band], turned[:, k * band : (k + 1) * band],
+                bias[jnp.where(r == bands - 1, 2, 1)], second, rows_second, heads,
             )
             for k, r in enumerate(places)
         ]

time: 22.3 us -> 22.8 us (1.022)
  Pallas kernels: 21.3 us -> 21.8 us
    pallas_call x1, Pallas kernels: 21.3 us -> 21.8 us  [on_device(): pl.pallas_call(functools.partial(kernel, ny, nx, height, breadth), out_sh...]
where the time goes in v5:
time: 22.8 us; the launch traced here: 22.6 us
  Pallas kernels  21.8 us (96%)
  local copies, waits for them, and re-layouts  0.8 us (4%)
    pallas_call x1, Pallas kernels, on_device(): pl.pallas_call(functools.partial(kernel, ny, nx, height, breadth), out_sh...  21.8 us
    unnamed x1, local copies, waits for them, and re-layouts  0.8 us

profile of v5, /device:TPU:0, one launch (start us, length us, event | category | flops | bytes accessed | tf_op | source)
XLA Modules:
  0.0 22.6 jit_solution(8581947018466533461)
XLA Ops:
  0.0 21.8 %shard_map.82 = f32[64,16,128]{2,1,0:T(8,128)S(1)} custom-call(bf16[64,16,128]{2,1,0:T(8,128)(2,1)} %feat_in.1, f32[2,128]{1,0:T(2,128)} %again_in.1, bf16[2,128,384]{2,1,0:T(8,128)(2,1)} %tw_in.1, bf16[2,128,128]{2,1,0:T(8,128)(2,1)} %ow_in.1, f32[2,4,225]{2,1,0:T(4,128)} %table_in.1, f32[2,128]{1,0:T(2,128)} %hgain_in.1, bf16[2,128,512]{2,1,0:T(8,128)(2,1)} %ew_in.1, ...), custom_call_target="tpu_custom_call" | custom-call | flops 1000000000 | bytes 2000000 | tf_op jit(solution)/shard_map/pallas_call | solution.py:339
  21.8 0.8 %copy.10 = f32[64,16,128]{2,1,0:T(8,128)} copy(f32[64,16,128]{2,1,0:T(8,128)S(1)} %shard_map.82) | data formatting | bytes 1048576

commit v6 on v4

--- a/solution.py
+++ b/solution.py
@@ -102,12 +102,18 @@
     )
     first_half = lax.broadcasted_iota(jnp.int32, (WIN, 4 * WIN * WIN), 1) & 15 < WIN
     loads[0].wait()
-    spread_rows = [
-        jnp.dot(table[b], pick, precision=lax.Precision.HIGHEST, preferred_element_type=F32) for b in range(2)
-    ]
+    rest = jnp.concatenate([table[0], table[1]], axis=0)
+    terms = []
+    for _ in range(3):
+        terms.append(rest.astype(BF16).astype(F32))
+        rest = rest - terms[-1]
+    found = jnp.dot(
+        jnp.concatenate(terms, axis=0).astype(BF16), pick.astype(BF16), preferred_element_type=F32
+    )
+    picked = found[:WIN] + found[WIN : 2 * WIN] + found[2 * WIN :]
     for b in range(2):
         for h in range(HEADS):
-            row = jnp.broadcast_to(spread_rows[b][h : h + 1], (WIN, 4 * WIN * WIN))
+            row = jnp.broadcast_to(picked[b * HEADS + h : b * HEADS + h + 1], (WIN, 4 * WIN * WIN))
             rows = jnp.where(
                 first_half,
                 pltpu.roll(row, 4 * WIN * WIN - WIN + 1, 1, stride=1, stride_axis=0),

time: 22.3 us -> 22.2 us (level)
  no operation moved by 1% of the time
where the time goes in v6:
time: 22.2 us; the launch traced here: 22 us
  Pallas kernels  21.2 us (95%)
  local copies, waits for them, and re-layouts  0.8 us (4%)
    pallas_call x1, Pallas kernels, on_device(): pl.pallas_call(functools.partial(kernel, ny, nx, height, breadth), out_sh...  21.2 us
    unnamed x1, local copies, waits for them, and re-layouts  0.8 us

profile of v6, /device:TPU:0, one launch (start us, length us, event | category | flops | bytes accessed | tf_op | source)
XLA Modules:
  0.0 22.0 jit_solution(8342102923091544043)
XLA Ops:
  0.0 21.2 %shard_map.82 = f32[64,16,128]{2,1,0:T(8,128)S(1)} custom-call(bf16[64,16,128]{2,1,0:T(8,128)(2,1)} %feat_in.1, f32[2,128]{1,0:T(2,128)} %again_in.1, bf16[2,128,384]{2,1,0:T(8,128)(2,1)} %tw_in.1, bf16[2,128,128]{2,1,0:T(8,128)(2,1)} %ow_in.1, f32[2,4,225]{2,1,0:T(4,128)} %table_in.1, f32[2,128]{1,0:T(2,128)} %hgain_in.1, bf16[2,128,512]{2,1,0:T(8,128)(2,1)} %ew_in.1, ...), custom_call_target="tpu_custom_call" | custom-call | flops 1000000000 | bytes 2000000 | tf_op jit(solution)/shard_map/pallas_call | solution.py:338
  21.2 0.8 %copy.10 = f32[64,16,128]{2,1,0:T(8,128)} copy(f32[64,16,128]{2,1,0:T(8,128)S(1)} %shard_map.82) | data formatting | bytes 1048576
